TPU v7x, 32 devices: a whole 2x2x4 slice. The times are simulated.
32 devices in a mesh: blk: 16 (over z, y, core), help: 2 (over x).
Axes of the slice: x: 2, y: 2, z: 4, core: 2. Of those that a mesh axis runs over, the one named last changes fastest.
Arguments:
- heads: float32 [4096, 400], P(('blk', 'help')), may hold values from -6 to 6
- tails: float32 [4096, 400], P(('blk', 'help')), may hold values from -6 to 6
- head_acc: float32 [4096], P(('blk', 'help')), may hold values from 0.01 to 0.1
- tail_acc: float32 [4096], P(('blk', 'help')), may hold values from 0.01 to 0.1
- relations: bfloat16 [7424, 400], replicated, may hold values from -0.59765625 to 0.59765625
- counts: int32 [4, 32], P(None, ('blk', 'help')), may hold values from 1 to 5, as said below
- rel_ids: int32 [4, 32, 5], P(None, ('blk', 'help')), may hold values from 0 to 7423
- head_edges: int32 [4, 32, 5, 1024], P(None, ('blk', 'help')), may hold values from 0 to 127
- tail_edges: int32 [4, 32, 5, 1024], P(None, ('blk', 'help')), may hold values from 0 to 127
Outputs:
- new_heads: float32 [4096, 400], P(('blk', 'help'))
- new_tails: float32 [4096, 400], P(('blk', 'help'))
- new_head_acc: float32 [4096], P(('blk', 'help'))
- new_tail_acc: float32 [4096], P(('blk', 'help'))
Inputs may be any that keep to these rules, and one draw needn't show every extreme that they name: `counts`: in every round the two partitions 2 q and 2 q + 1 have one count from 3 to 5 and the other 1 or 2; in every round partitions 0 and 1 hold 5 and 1.
All inputs are finite; a program needn't handle non-finite values.
Results may differ from a plain program's by a relative error of at most 0.0003.
Values sent between devices are 32-bit elements; how exact they have to be, the bound alone decides.
A program may use at most 64 MiB of HBM per device.

v0:
```python
import functools

import jax
import jax.numpy as jnp
from jax import lax
from jax.experimental import pallas as pl
from jax.experimental.pallas import tpu as pltpu
from jax.sharding import PartitionSpec as P

NEG_WEIGHT = 0.0625
LEARN_RATE = 0.1
LANES = 128
SUBLANES = 8
FIRST_PART = 256
TABLE_PARTS = 4
VMEM_BYTES = 60 * 1024 * 1024
NT = (((1,), (1,)), ((), ()))
NN = (((1,), (0,)), ((), ()))


def split(value):
    high = value.astype(jnp.bfloat16)
    return high, (value - high.astype(jnp.float32)).astype(jnp.bfloat16)


def dot(left, right, dims=NN):
    return lax.dot_general(left, right, dims, preferred_element_type=jnp.float32)


def product(left, right):
    return dot(left[0], right[0]) + (dot(left[0], right[1]) + dot(left[1], right[0]))


def task(s, rows):
    return slice(s * rows, (s + 1) * rows)


def one_hot(index, rows):
    row_of = lax.broadcasted_iota(jnp.int32, (rows, index.shape[1]), 0)
    same = row_of.astype(jnp.bfloat16) == index.astype(jnp.bfloat16)
    return jnp.where(same, jnp.bfloat16(1.0), jnp.bfloat16(0.0))


def label_counts(head_index, tail_index, rows):
    return dot(one_hot(tail_index, rows), one_hot(head_index, rows), NT)


def kernel(
    blk_size,
    heads_ref,
    tails_ref,
    head_acc_ref,
    tail_acc_ref,
    counts_ref,
    rel_ids_ref,
    head_edges_ref,
    tail_edges_ref,
    relations_hbm,
    new_heads_ref,
    new_tails_ref,
    new_head_acc_ref,
    new_tail_acc_ref,
    table,
    gathered,
    spread_rel,
    labels,
    scaled_high,
    scaled_low,
    arrived,
    leaving,
    table_sems,
    send_sem,
    recv_sem,
):
    width, rows = heads_ref.shape
    rounds = counts_ref.shape[1]
    slots = rel_ids_ref.shape[2]
    rels = table.shape[1]
    padded = width + SUBLANES
    parts = ((0, FIRST_PART), (FIRST_PART, padded))
    me = lax.axis_index("blk")

    def device(distance):
        return lax.rem(me + distance + blk_size, blk_size)

    step = pl.cdiv(rels, TABLE_PARTS * 2 * LANES) * 2 * LANES
    table_copies = []
    for at, start in enumerate(range(0, rels, step)):
        lanes = pl.ds(start, min(step, rels - start))
        copy = pltpu.make_async_copy(
            relations_hbm.at[:, lanes], table.at[:, lanes], table_sems.at[at]
        )
        copy.start()
        table_copies.append(copy)

    barrier = pltpu.get_barrier_semaphore()
    partners = (1, -1, rounds - 1, 1 - rounds)
    for distance in partners:
        pl.semaphore_signal(
            barrier,
            inc=1,
            device_id={"blk": device(distance)},
            device_id_type=pl.DeviceIdType.MESH,
        )

    def store_labels(k):
        for s in range(slots):
            at = k * slots + s
            labels[:, task(s, rows)] = label_counts(head_edges_ref[at], tail_edges_ref[at], rows)

    def gather_relations():
        lane = lax.broadcasted_iota(jnp.int32, (1, LANES), 1)
        wanted = jnp.full((1, LANES), -1, jnp.int32)
        for at in range(rounds * slots):
            rel_id = rel_ids_ref[at // slots, :, at % slots : at % slots + 1]
            wanted = jnp.where(lane == at, rel_id, wanted)
        total = jnp.zeros(gathered.shape, jnp.float32)
        for at, start in enumerate(range(0, rels, step)):
            size = min(step, rels - start)
            rel_of = lax.broadcasted_iota(jnp.int32, (size, LANES), 0) + start
            pick = jnp.where(rel_of == wanted, 1.0, 0.0).astype(jnp.bfloat16)
            table_copies[at].wait()
            total = total + dot(table[:, start : start + size], pick)
        gathered[...] = total.astype(jnp.bfloat16)

    def store_scaled(k, head_block):
        lane_of = lax.broadcasted_iota(jnp.int32, (LANES, slots * rows), 0)
        task_of = lax.broadcasted_iota(jnp.int32, (LANES, slots * rows), 1) // rows
        pick = jnp.where(lane_of == k * slots + task_of, 1.0, 0.0).astype(jnp.bfloat16)
        spread = dot(gathered[...], pick)
        spread_rel[k % 2] = spread
        for s in range(slots):
            high, low = split(head_block * spread[:, task(s, rows)])
            scaled_high[:, task(s, rows)] = high
            scaled_low[:, task(s, rows)] = low

    def state_after(state, grad):
        return state + jnp.sum(grad * grad, axis=0, keepdims=True) * (1.0 / width)

    store_labels(0)
    gather_relations()
    store_scaled(0, heads_ref[...])
    head_state = head_acc_ref[...]
    pl.semaphore_wait(barrier, len(partners))

    copies = []
    for k in range(rounds):
        scores = None
        pieces = []
        for at, (start, stop) in enumerate(parts):
            end = min(stop, width)
            if k == 0:
                piece = tails_ref[start:end, :]
            else:
                copies[2 * (k - 1) + at].wait_recv()
                piece = arrived[k - 1, start:end, :]
            scaled_part = (scaled_high[start:end, :], scaled_low[start:end, :])
            partial = product(split(jnp.transpose(piece)), scaled_part)
            scores = partial if scores is None else scores + partial
            pieces.append(piece)
        tail_state = tail_acc_ref[...] if k == 0 else arrived[k - 1, width : width + 1, :]
        task_of = lax.broadcasted_iota(jnp.int32, (1, slots * rows), 1) // rows
        active = jnp.where(task_of < counts_ref[:, k : k + 1], 1.0, 0.0)
        weight = active * (0.5 * NEG_WEIGHT)
        coefficient = weight * jnp.tanh(0.5 * scores) + (weight - active * labels[...])
        high, low = split(coefficient)
        both = dot(scaled_high[...], jnp.concatenate([high, low], axis=0), NT)
        tail_grad = both[:, :rows] + (both[:, rows:] + dot(scaled_low[...], high, NT))
        tail_state = state_after(tail_state, tail_grad)
        rate = LEARN_RATE / jnp.sqrt(tail_state)
        for at, (start, stop) in enumerate(parts):
            end = min(stop, width)
            leaving[k, start:end, :] = pieces[at] - tail_grad[start:end] * rate
            if stop > width:
                leaving[k, width:, :] = jnp.broadcast_to(tail_state, (SUBLANES, rows))
            copy = pltpu.make_async_remote_copy(
                src_ref=leaving.at[k, pl.ds(start, stop - start)],
                dst_ref=arrived.at[k, pl.ds(start, stop - start)],
                send_sem=send_sem.at[k, at],
                recv_sem=recv_sem.at[k, at],
                device_id={"blk": device(1 if k < rounds - 1 else 1 - rounds)},
                device_id_type=pl.DeviceIdType.MESH,
            )
            copy.start()
            copies.append(copy)

        tail_high, tail_low = split(jnp.concatenate(pieces, axis=0))
        wide = jnp.concatenate([tail_high, tail_low, tail_high], axis=1)
        tall = jnp.concatenate([high, high, low], axis=0)
        weighted = dot(wide, tall) * spread_rel[k % 2]
        head_grad = weighted[:, task(0, rows)]
        for s in range(1, slots):
            head_grad = head_grad + weighted[:, task(s, rows)]
        old_head = heads_ref[...] if k == 0 else new_heads_ref[...]
        head_state = state_after(head_state, head_grad)
        new_head = old_head - head_grad * (LEARN_RATE / jnp.sqrt(head_state))
        new_heads_ref[...] = new_head
        if k < rounds - 1:
            store_scaled(k + 1, new_head)
            store_labels(k + 1)

    new_head_acc_ref[...] = head_state
    for copy in copies[-2:]:
        copy.wait_recv()
    new_tails_ref[...] = arrived[rounds - 1, :width, :]
    new_tail_acc_ref[...] = arrived[rounds - 1, width : width + 1, :]
    for copy in copies:
        copy.wait_send()


def write_out(*refs):
    count = (len(refs) - 2) // 3
    sems_in, sems_out = refs[-2:]
    copies_in = []
    copies_out = []
    for at in range(count):
        near = refs[2 * count + at]
        copies_in.append(pltpu.make_async_copy(refs[at], near, sems_in.at[at]))
        copies_out.append(pltpu.make_async_copy(near, refs[count + at], sems_out.at[at]))
        copies_in[at].start()
    for at in range(count):
        copies_in[at].wait()
        copies_out[at].start()
    for copy in copies_out:
        copy.wait()


def on_device(
    blk_size, heads, tails, head_acc, tail_acc, relations, counts, rel_ids, head_edges, tail_edges
):
    rows, width = heads.shape
    rounds, _, slots, edges = head_edges.shape
    vmem = pl.BlockSpec(memory_space=pltpu.VMEM)
    hbm = pl.BlockSpec(memory_space=pltpu.HBM)
    block = jax.ShapeDtypeStruct((width, rows), jnp.float32)
    line = jax.ShapeDtypeStruct((1, rows), jnp.float32)
    head_edges = head_edges.reshape(rounds * slots, 1, edges)
    tail_edges = tail_edges.reshape(rounds * slots, 1, edges)
    results = pl.pallas_call(
        functools.partial(kernel, blk_size),
        out_shape=(block, block, line, line),
        in_specs=[vmem] * 8 + [hbm],
        out_specs=(vmem,) * 4,
        scratch_shapes=[
            pltpu.VMEM(relations.shape[::-1], jnp.bfloat16),
            pltpu.VMEM((width, LANES), jnp.bfloat16),
            pltpu.VMEM((2, width, slots * rows), jnp.float32),
            pltpu.VMEM((rows, slots * rows), jnp.float32),
            pltpu.VMEM((width, slots * rows), jnp.bfloat16),
            pltpu.VMEM((width, slots * rows), jnp.bfloat16),
            pltpu.VMEM((rounds, width + SUBLANES, rows), jnp.float32),
            pltpu.VMEM((rounds, width + SUBLANES, rows), jnp.float32),
            pltpu.SemaphoreType.DMA((TABLE_PARTS,)),
            pltpu.SemaphoreType.DMA((rounds, 2)),
            pltpu.SemaphoreType.DMA((rounds, 2)),
        ],
        compiler_params=pltpu.CompilerParams(
            collective_id=0, has_side_effects=True, vmem_limit_bytes=VMEM_BYTES
        ),
    )(
        heads.T,
        tails.T,
        head_acc.reshape(1, rows),
        tail_acc.reshape(1, rows),
        counts.T,
        rel_ids,
        head_edges,
        tail_edges,
        relations.T,
    )
    new_heads, new_tails, new_head_acc, new_tail_acc = pl.pallas_call(
        write_out,
        out_shape=(block, block, line, line),
        in_specs=[hbm] * 4,
        out_specs=(hbm,) * 4,
        scratch_shapes=[
            pltpu.VMEM((width, rows), jnp.float32),
            pltpu.VMEM((width, rows), jnp.float32),
            pltpu.VMEM((1, rows), jnp.float32),
            pltpu.VMEM((1, rows), jnp.float32),
            pltpu.SemaphoreType.DMA((4,)),
            pltpu.SemaphoreType.DMA((4,)),
        ],
        compiler_params=pltpu.CompilerParams(vmem_limit_bytes=VMEM_BYTES),
    )(*results)
    return (new_heads.T, new_tails.T, new_head_acc.reshape(rows), new_tail_acc.reshape(rows))


def solution(mesh):
    both = ("blk", "help")
    in_specs = (
        P(both, None),
        P(both, None),
        P(both),
        P(both),
        P(),
        P(None, both),
        P(None, both, None),
        P(None, both, None, None),
        P(None, both, None, None),
    )
    out_specs = (P(both, None), P(both, None), P(both), P(both))
    return jax.shard_map(
        functools.partial(on_device, mesh.shape["blk"]),
        mesh=mesh,
        in_specs=in_specs,
        out_specs=out_specs,
        check_vma=False,
    )
```

profile of v0, /device:TPU:29, one launch (start us, length us, event | category | flops | bytes accessed | tf_op | source)
XLA Modules:
  0.0 33.6 jit_solution(16626304801270182411)
XLA Ops:
  0.6 31.1 %shard_map.120 = (f32[400,128]{1,0:T(8,128)}, f32[400,128]{1,0:T(8,128)}, f32[1,128]{1,0:T(1,128)}, f32[1,128]{1,0:T(1,128)}) custom-call(f32[400,128]{1,0:T(8,128)} %bitcast.13, f32[400,128]{1,0:T(8,128)} %bitcast.14, f32[1,128]{1,0:T(1,128)} %bitcast.17, f32[1,128]{1,0:T(1,128)} %bitcast.18, s32[1,4]{1,0:T(1,128)} %bitcast.19, s32[4,1,5]{2,1,0:T(1,128)} %rel_ids_ref.1, ...), custom_call_target="tpu_custom_call" | custom-call | tf_op jit(solution)/shard_map/pallas_call | solution.py:239
  31.8 1.8 %shard_map.121 = (f32[400,128]{1,0:T(8,128)}, f32[400,128]{1,0:T(8,128)}, f32[1,128]{1,0:T(1,128)}, f32[1,128]{1,0:T(1,128)}) custom-call(f32[400,128]{1,0:T(8,128)} %get-tuple-element.12.refs_0_, f32[400,128]{1,0:T(8,128)} %get-tuple-element.13.refs_1_, f32[1,128]{1,0:T(1,128)} %get-tuple-element.14.refs_2_, f32[1,128]{1,0:T(1,128)} %get-tuple-element.15.refs_3_), custom_call_target="tpu_custom_call" | custom-call | tf_op jit(solution)/shard_map/pallas_call | solution.py:271
where the time goes:
time: 33.7 us; the launch traced here: 33.6 us
  Pallas kernels  32.9 us (98%)
  between operations  0.64 us (2%)
    pallas_call x1, Pallas kernels, on_device(): pl.pallas_call(functools.partial(kernel, blk_size), out_shape=(block, blo...  31.1 us
    pallas_call x1, Pallas kernels, on_device(): pl.pallas_call(write_out, out_shape=(block, block, line, line), in_specs=...  1.78 us

commit v1 on v0

--- a/solution.py
+++ b/solution.py
@@ -27,10 +27,6 @@
     return lax.dot_general(left, right, dims, preferred_element_type=jnp.float32)
 
 
-def product(left, right):
-    return dot(left[0], right[0]) + (dot(left[0], right[1]) + dot(left[1], right[0]))
-
-
 def task(s, rows):
     return slice(s * rows, (s + 1) * rows)
 
@@ -42,7 +38,7 @@
 
 
 def label_counts(head_index, tail_index, rows):
-    return dot(one_hot(tail_index, rows), one_hot(head_index, rows), NT)
+    return dot(one_hot(head_index, rows), one_hot(tail_index, rows), NT)
 
 
 def kernel(
@@ -62,8 +58,11 @@
     new_tail_acc_ref,
     table,
     gathered,
+    gathered_turned,
+    turned_high,
+    turned_low,
     spread_rel,
-    labels,
+    shifted_labels,
     scaled_high,
     scaled_low,
     arrived,
@@ -106,7 +105,9 @@
     def store_labels(k):
         for s in range(slots):
             at = k * slots + s
-            labels[:, task(s, rows)] = label_counts(head_edges_ref[at], tail_edges_ref[at], rows)
+            counted = label_counts(head_edges_ref[at], tail_edges_ref[at], rows)
+            kept = jnp.where(counts_ref[:, k : k + 1] > s, 1.0, 0.0)
+            shifted_labels[task(s, rows), :] = kept * (0.5 * NEG_WEIGHT - counted)
 
     def gather_relations():
         lane = lax.broadcasted_iota(jnp.int32, (1, LANES), 1)
@@ -122,6 +123,7 @@
             table_copies[at].wait()
             total = total + dot(table[:, start : start + size], pick)
         gathered[...] = total.astype(jnp.bfloat16)
+        gathered_turned[...] = jnp.transpose(total)
 
     def store_scaled(k, head_block):
         lane_of = lax.broadcasted_iota(jnp.int32, (LANES, slots * rows), 0)
@@ -133,6 +135,12 @@
             high, low = split(head_block * spread[:, task(s, rows)])
             scaled_high[:, task(s, rows)] = high
             scaled_low[:, task(s, rows)] = low
+        head_turned = jnp.transpose(head_block)
+        for s in range(slots):
+            at = k * slots + s
+            high, low = split(head_turned * gathered_turned[at : at + 1, :])
+            turned_high[task(s, rows), :] = high
+            turned_low[task(s, rows), :] = low
 
     def state_after(state, grad):
         return state + jnp.sum(grad * grad, axis=0, keepdims=True) * (1.0 / width)
@@ -154,18 +162,19 @@
             else:
                 copies[2 * (k - 1) + at].wait_recv()
                 piece = arrived[k - 1, start:end, :]
-            scaled_part = (scaled_high[start:end, :], scaled_low[start:end, :])
-            partial = product(split(jnp.transpose(piece)), scaled_part)
+            high, low = split(piece)
+            wide = dot(turned_high[:, start:end], jnp.concatenate([high, low], axis=1))
+            partial = wide[:, :rows] + (wide[:, rows:] + dot(turned_low[:, start:end], high))
             scores = partial if scores is None else scores + partial
             pieces.append(piece)
         tail_state = tail_acc_ref[...] if k == 0 else arrived[k - 1, width : width + 1, :]
-        task_of = lax.broadcasted_iota(jnp.int32, (1, slots * rows), 1) // rows
+        task_of = lax.broadcasted_iota(jnp.int32, (slots * rows, 1), 0) // rows
         active = jnp.where(task_of < counts_ref[:, k : k + 1], 1.0, 0.0)
         weight = active * (0.5 * NEG_WEIGHT)
-        coefficient = weight * jnp.tanh(0.5 * scores) + (weight - active * labels[...])
+        coefficient = weight * jnp.tanh(0.5 * scores) + shifted_labels[...]
         high, low = split(coefficient)
-        both = dot(scaled_high[...], jnp.concatenate([high, low], axis=0), NT)
-        tail_grad = both[:, :rows] + (both[:, rows:] + dot(scaled_low[...], high, NT))
+        both = dot(scaled_high[...], jnp.concatenate([high, low], axis=1))
+        tail_grad = both[:, :rows] + (both[:, rows:] + dot(scaled_low[...], high))
         tail_state = state_after(tail_state, tail_grad)
         rate = LEARN_RATE / jnp.sqrt(tail_state)
         for at, (start, stop) in enumerate(parts):
@@ -186,8 +195,8 @@
 
         tail_high, tail_low = split(jnp.concatenate(pieces, axis=0))
         wide = jnp.concatenate([tail_high, tail_low, tail_high], axis=1)
-        tall = jnp.concatenate([high, high, low], axis=0)
-        weighted = dot(wide, tall) * spread_rel[k % 2]
+        mixed = jnp.concatenate([high, high, low], axis=1)
+        weighted = dot(wide, mixed, NT) * spread_rel[k % 2]
         head_grad = weighted[:, task(0, rows)]
         for s in range(1, slots):
             head_grad = head_grad + weighted[:, task(s, rows)]
@@ -244,8 +253,11 @@
         scratch_shapes=[
             pltpu.VMEM(relations.shape[::-1], jnp.bfloat16),
             pltpu.VMEM((width, LANES), jnp.bfloat16),
+            pltpu.VMEM((LANES, width), jnp.float32),
+            pltpu.VMEM((slots * rows, width), jnp.bfloat16),
+            pltpu.VMEM((slots * rows, width), jnp.bfloat16),
             pltpu.VMEM((2, width, slots * rows), jnp.float32),
-            pltpu.VMEM((rows, slots * rows), jnp.float32),
+            pltpu.VMEM((slots * rows, rows), jnp.float32),
             pltpu.VMEM((width, slots * rows), jnp.bfloat16),
             pltpu.VMEM((width, slots * rows), jnp.bfloat16),
             pltpu.VMEM((rounds, width + SUBLANES, rows), jnp.float32),

time: 33.7 us -> 33.2 us (0.985)
  Pallas kernels: 32.9 us -> 32.4 us
    pallas_call x1, Pallas kernels: 31.1 us -> 30.6 us  [on_device(): pl.pallas_call(functools.partial(kernel, blk_size), out_shape=(block, blo...]
where the time goes in v1:
time: 33.2 us; the launch traced here: 33 us
  Pallas kernels  32.4 us (98%)
  between operations  0.64 us (2%)
    pallas_call x1, Pallas kernels, on_device(): pl.pallas_call(functools.partial(kernel, blk_size), out_shape=(block, blo...  30.6 us
    pallas_call x1, Pallas kernels, on_device(): pl.pallas_call(write_out, out_shape=(block, block, line, line), in_specs=...  1.78 us

profile of v1, /device:TPU:29, one launch (start us, length us, event | category | flops | bytes accessed | tf_op | source)
XLA Modules:
  0.0 33.0 jit_solution(18345652454690523048)
XLA Ops:
  0.6 30.6 %shard_map.120 = (f32[400,128]{1,0:T(8,128)}, f32[400,128]{1,0:T(8,128)}, f32[1,128]{1,0:T(1,128)}, f32[1,128]{1,0:T(1,128)}) custom-call(f32[400,128]{1,0:T(8,128)} %bitcast.13, f32[400,128]{1,0:T(8,128)} %bitcast.14, f32[1,128]{1,0:T(1,128)} %bitcast.17, f32[1,128]{1,0:T(1,128)} %bitcast.18, s32[1,4]{1,0:T(1,128)} %bitcast.19, s32[4,1,5]{2,1,0:T(1,128)} %rel_ids_ref.1, ...), custom_call_target="tpu_custom_call" | custom-call | tf_op jit(solution)/shard_map/pallas_call | solution.py:248
  31.3 1.8 %shard_map.121 = (f32[400,128]{1,0:T(8,128)}, f32[400,128]{1,0:T(8,128)}, f32[1,128]{1,0:T(1,128)}, f32[1,128]{1,0:T(1,128)}) custom-call(f32[400,128]{1,0:T(8,128)} %get-tuple-element.12.refs_0_, f32[400,128]{1,0:T(8,128)} %get-tuple-element.13.refs_1_, f32[1,128]{1,0:T(1,128)} %get-tuple-element.14.refs_2_, f32[1,128]{1,0:T(1,128)} %get-tuple-element.15.refs_3_), custom_call_target="tpu_custom_call" | custom-call | tf_op jit(solution)/shard_map/pallas_call | solution.py:283

commit v2 on v1

--- a/solution.py
+++ b/solution.py
@@ -43,6 +43,19 @@
 
 def kernel(
     blk_size,
+    heads_hbm,
+    tails_hbm,
+    head_acc_hbm,
+    tail_acc_hbm,
+    counts_hbm,
+    rel_ids_hbm,
+    head_edges_hbm,
+    tail_edges_hbm,
+    relations_hbm,
+    new_heads_hbm,
+    new_tails_hbm,
+    new_head_acc_hbm,
+    new_tail_acc_hbm,
     heads_ref,
     tails_ref,
     head_acc_ref,
@@ -51,9 +64,7 @@
     rel_ids_ref,
     head_edges_ref,
     tail_edges_ref,
-    relations_hbm,
     new_heads_ref,
-    new_tails_ref,
     new_head_acc_ref,
     new_tail_acc_ref,
     table,
@@ -67,6 +78,8 @@
     scaled_low,
     arrived,
     leaving,
+    input_sems,
+    output_sems,
     table_sems,
     send_sem,
     recv_sem,
@@ -81,6 +94,22 @@
 
     def device(distance):
         return lax.rem(me + distance + blk_size, blk_size)
+
+    inputs = (
+        (rel_ids_hbm, rel_ids_ref),
+        (counts_hbm, counts_ref),
+        (head_edges_hbm, head_edges_ref),
+        (tail_edges_hbm, tail_edges_ref),
+        (heads_hbm, heads_ref),
+        (tails_hbm, tails_ref),
+        (head_acc_hbm, head_acc_ref),
+        (tail_acc_hbm, tail_acc_ref),
+    )
+    input_copies = []
+    for at, (source, target) in enumerate(inputs):
+        copy = pltpu.make_async_copy(source, target, input_sems.at[at])
+        copy.start()
+        input_copies.append(copy)
 
     step = pl.cdiv(rels, TABLE_PARTS * 2 * LANES) * 2 * LANES
     table_copies = []
@@ -145,8 +174,12 @@
     def state_after(state, grad):
         return state + jnp.sum(grad * grad, axis=0, keepdims=True) * (1.0 / width)
 
+    for copy in input_copies[:4]:
+        copy.wait()
     store_labels(0)
     gather_relations()
+    for copy in input_copies[4:]:
+        copy.wait()
     store_scaled(0, heads_ref[...])
     head_state = head_acc_ref[...]
     pl.semaphore_wait(barrier, len(partners))
@@ -209,10 +242,25 @@
             store_labels(k + 1)
 
     new_head_acc_ref[...] = head_state
-    for copy in copies[-2:]:
-        copy.wait_recv()
-    new_tails_ref[...] = arrived[rounds - 1, :width, :]
+    outputs = [(new_heads_ref, new_heads_hbm), (new_head_acc_ref, new_head_acc_hbm)]
+    for start, stop in parts:
+        span = pl.ds(start, min(stop, width) - start)
+        outputs.append((arrived.at[rounds - 1, span], new_tails_hbm.at[span]))
+    outputs.append((new_tail_acc_ref, new_tail_acc_hbm))
+    output_copies = [
+        pltpu.make_async_copy(source, target, output_sems.at[at])
+        for at, (source, target) in enumerate(outputs)
+    ]
+    output_copies[0].start()
+    output_copies[1].start()
+    copies[-2].wait_recv()
+    output_copies[2].start()
+    copies[-1].wait_recv()
+    output_copies[3].start()
     new_tail_acc_ref[...] = arrived[rounds - 1, width : width + 1, :]
+    output_copies[4].start()
+    for copy in output_copies:
+        copy.wait()
     for copy in copies:
         copy.wait_send()
 
@@ -239,7 +287,6 @@
 ):
     rows, width = heads.shape
     rounds, _, slots, edges = head_edges.shape
-    vmem = pl.BlockSpec(memory_space=pltpu.VMEM)
     hbm = pl.BlockSpec(memory_space=pltpu.HBM)
     block = jax.ShapeDtypeStruct((width, rows), jnp.float32)
     line = jax.ShapeDtypeStruct((1, rows), jnp.float32)
@@ -248,9 +295,20 @@
     results = pl.pallas_call(
         functools.partial(kernel, blk_size),
         out_shape=(block, block, line, line),
-        in_specs=[vmem] * 8 + [hbm],
-        out_specs=(vmem,) * 4,
+        in_specs=[hbm] * 9,
+        out_specs=(hbm,) * 4,
         scratch_shapes=[
+            pltpu.VMEM((width, rows), jnp.float32),
+            pltpu.VMEM((width, rows), jnp.float32),
+            pltpu.VMEM((1, rows), jnp.float32),
+            pltpu.VMEM((1, rows), jnp.float32),
+            pltpu.VMEM((1, rounds), jnp.int32),
+            pltpu.VMEM(rel_ids.shape, jnp.int32),
+            pltpu.VMEM(head_edges.shape, jnp.int32),
+            pltpu.VMEM(tail_edges.shape, jnp.int32),
+            pltpu.VMEM((width, rows), jnp.float32),
+            pltpu.VMEM((1, rows), jnp.float32),
+            pltpu.VMEM((1, rows), jnp.float32),
             pltpu.VMEM(relations.shape[::-1], jnp.bfloat16),
             pltpu.VMEM((width, LANES), jnp.bfloat16),
             pltpu.VMEM((LANES, width), jnp.float32),
@@ -262,6 +320,8 @@
             pltpu.VMEM((width, slots * rows), jnp.bfloat16),
             pltpu.VMEM((rounds, width + SUBLANES, rows), jnp.float32),
             pltpu.VMEM((rounds, width + SUBLANES, rows), jnp.float32),
+            pltpu.SemaphoreType.DMA((8,)),
+            pltpu.SemaphoreType.DMA((5,)),
             pltpu.SemaphoreType.DMA((TABLE_PARTS,)),
             pltpu.SemaphoreType.DMA((rounds, 2)),
             pltpu.SemaphoreType.DMA((rounds, 2)),

time: 33.2 us -> 32.5 us (0.979)
  Pallas kernels: 32.4 us -> 31.7 us
    pallas_call x1, Pallas kernels: 30.6 us -> 29.9 us  [on_device(): pl.pallas_call(functools.partial(kernel, blk_size), out_shape=(block, blo...]
where the time goes in v2:
time: 32.5 us; the launch traced here: 32.3 us
  Pallas kernels  31.7 us (98%)
  between operations  0.64 us (2%)
    pallas_call x1, Pallas kernels, on_device(): pl.pallas_call(functools.partial(kernel, blk_size), out_shape=(block, blo...  29.9 us
    pallas_call x1, Pallas kernels, on_device(): pl.pallas_call(write_out, out_shape=(block, block, line, line), in_specs=...  1.78 us

profile of v2, /device:TPU:29, one launch (start us, length us, event | category | flops | bytes accessed | tf_op | source)
XLA Modules:
  0.0 32.3 jit_solution(4402421948461314368)
XLA Ops:
  0.6 29.9 %shard_map.120 = (f32[400,128]{1,0:T(8,128)}, f32[400,128]{1,0:T(8,128)}, f32[1,128]{1,0:T(1,128)}, f32[1,128]{1,0:T(1,128)}) custom-call(f32[400,128]{1,0:T(8,128)} %bitcast.13, f32[400,128]{1,0:T(8,128)} %bitcast.14, f32[1,128]{1,0:T(1,128)} %bitcast.17, f32[1,128]{1,0:T(1,128)} %bitcast.18, s32[1,4]{1,0:T(1,128)} %bitcast.19, s32[4,1,5]{2,1,0:T(1,128)} %rel_ids_hbm.1, ...), custom_call_target="tpu_custom_call" | custom-call | tf_op jit(solution)/shard_map/pallas_call | solution.py:295
  30.5 1.8 %shard_map.121 = (f32[400,128]{1,0:T(8,128)}, f32[400,128]{1,0:T(8,128)}, f32[1,128]{1,0:T(1,128)}, f32[1,128]{1,0:T(1,128)}) custom-call(f32[400,128]{1,0:T(8,128)} %get-tuple-element.12.refs_0_, f32[400,128]{1,0:T(8,128)} %get-tuple-element.13.refs_1_, f32[1,128]{1,0:T(1,128)} %get-tuple-element.14.refs_2_, f32[1,128]{1,0:T(1,128)} %get-tuple-element.15.refs_3_), custom_call_target="tpu_custom_call" | custom-call | tf_op jit(solution)/shard_map/pallas_call | solution.py:343

commit v3 on v2

--- a/solution.py
+++ b/solution.py
@@ -12,7 +12,7 @@
 LANES = 128
 SUBLANES = 8
 FIRST_PART = 256
-TABLE_PARTS = 4
+TABLE_PARTS = 8
 VMEM_BYTES = 60 * 1024 * 1024
 NT = (((1,), (1,)), ((), ()))
 NN = (((1,), (0,)), ((), ()))

time: 32.5 us -> 32.7 us (level)
  no operation moved by 1% of the time
where the time goes in v3:
time: 32.7 us; the launch traced here: 32.6 us
  Pallas kernels  31.9 us (98%)
  between operations  0.64 us (2%)
    pallas_call x1, Pallas kernels, on_device(): pl.pallas_call(functools.partial(kernel, blk_size), out_shape=(block, blo...  30.1 us
    pallas_call x1, Pallas kernels, on_device(): pl.pallas_call(write_out, out_shape=(block, block, line, line), in_specs=...  1.78 us

profile of v3, /device:TPU:29, one launch (start us, length us, event | category | flops | bytes accessed | tf_op | source)
XLA Modules:
  0.0 32.6 jit_solution(14217199609744243985)
XLA Ops:
  0.6 30.1 %shard_map.120 = (f32[400,128]{1,0:T(8,128)}, f32[400,128]{1,0:T(8,128)}, f32[1,128]{1,0:T(1,128)}, f32[1,128]{1,0:T(1,128)}) custom-call(f32[400,128]{1,0:T(8,128)} %bitcast.13, f32[400,128]{1,0:T(8,128)} %bitcast.14, f32[1,128]{1,0:T(1,128)} %bitcast.17, f32[1,128]{1,0:T(1,128)} %bitcast.18, s32[1,4]{1,0:T(1,128)} %bitcast.19, s32[4,1,5]{2,1,0:T(1,128)} %rel_ids_hbm.1, ...), custom_call_target="tpu_custom_call" | custom-call | tf_op jit(solution)/shard_map/pallas_call | solution.py:295
  30.8 1.8 %shard_map.121 = (f32[400,128]{1,0:T(8,128)}, f32[400,128]{1,0:T(8,128)}, f32[1,128]{1,0:T(1,128)}, f32[1,128]{1,0:T(1,128)}) custom-call(f32[400,128]{1,0:T(8,128)} %get-tuple-element.12.refs_0_, f32[400,128]{1,0:T(8,128)} %get-tuple-element.13.refs_1_, f32[1,128]{1,0:T(1,128)} %get-tuple-element.14.refs_2_, f32[1,128]{1,0:T(1,128)} %get-tuple-element.15.refs_3_), custom_call_target="tpu_custom_call" | custom-call | tf_op jit(solution)/shard_map/pallas_call | solution.py:343
